TPU v7x, 32 devices: a whole 2x2x4 slice. The times are simulated.
32 devices in a mesh: req: 16 (over z, x, core), ctx: 2 (over y).
Axes of the slice: x: 2, y: 2, z: 4, core: 2. Of those that a mesh axis runs over, the one named last changes fastest.
Arguments:
- q_heads: bfloat16 [16, 256, 12288], P('req', 'ctx'), may hold values from -204 to 204
- kv_latent: bfloat16 [16, 256, 576], P('req', 'ctx'), may hold values from -600 to 600
- latent_gain: float32 [512], replicated, may hold values from 0.1 to 1.9
- kv_up: bfloat16 [64, 256, 512], P('ctx'), may hold values from -0.25 to 0.25
- offsets: int32 [16], P('req'), may hold values from 0 to 1792, as said below
- lengths: int32 [16], P('req'), may hold values from 64 to 256
- block_order: int32 [16, 4], P('req'), may hold values from 0 to 3, each once within a row
- owners: int32 [16, 4], P(None, 'ctx'), may hold values from 0 to 15, as said below
Outputs:
- attn_out: bfloat16 [16, 256, 8192], P('req', 'ctx')
- shipped: bfloat16 [16, 4, 36864], P('req', 'ctx')
Inputs may be any that keep to these rules, and one draw needn't show every extreme that they name: `offsets`: each entry is a multiple of 256. `block_order`: each row names every block index once. `owners`: for each context index j, column 2 j and column 2 j + 1 each name every owner once, and no row names the same owner in both of them.
All inputs are finite; a program needn't handle non-finite values.
Results may differ from a plain program's by a relative error of at most 0.007.
Values may be sent and summed in bfloat16 or wider, within the bound.
A program may use at most 64 MiB of HBM per device.

v0:
```python
import math

import jax
import jax.numpy as jnp
from jax import lax
from jax.sharding import PartitionSpec as P

HEADS = 64
HD = 128
ROPE = 64
LAT = 512


theta_base = 10000.0
epsilon = 1e-06
masked_fill = -1e30


def as_sent(array):
    return jax.tree.map(lambda a: a.astype(jnp.bfloat16) if a.dtype == jnp.float32 else a, array)


def rotate(values, angles):
    half_width = values.shape[-1] // 2
    first_half = values[..., :half_width]
    second_half = values[..., half_width:]
    cosine = jnp.cos(angles)
    sine_part = jnp.sin(angles)
    return jnp.concatenate(
        [
            first_half * cosine - second_half * sine_part,
            second_half * cosine + first_half * sine_part,
        ],
        axis=-1,
    )


def angle_table(positions, rope_width):
    half_width = rope_width // 2
    frequency = jnp.exp(
        -math.log(theta_base) * jnp.arange(half_width, dtype=jnp.float32) / half_width
    )
    return positions.astype(jnp.float32)[:, None] * frequency[None, :]


def make_cache(latent_rows, latent_gain, angles):
    latent = latent_rows[:, :LAT].astype(jnp.float32)
    mean_square = jnp.mean(latent * latent, axis=-1, keepdims=True)
    normed = (latent * lax.rsqrt(mean_square + epsilon) * latent_gain).astype(jnp.bfloat16)
    key_rope = rotate(latent_rows[:, LAT:].astype(jnp.float32), angles).astype(jnp.bfloat16)
    return jnp.concatenate([normed, key_rope], axis=-1)


def attend(queries, key_rows, value_weight, allowed, valid_rows):
    score_scale = (HD + ROPE) ** (-0.5)
    scores = (
        jnp.einsum("qc,kc->qk", queries, key_rows, preferred_element_type=jnp.float32) * score_scale
    )
    masked = jnp.where(allowed, scores, masked_fill)
    row_max = jnp.max(masked, axis=-1, keepdims=True)
    exponent = jnp.exp(masked - row_max)
    probabilities = (exponent / jnp.sum(exponent, axis=-1, keepdims=True)).astype(jnp.bfloat16)
    output_latent = jnp.dot(
        probabilities, key_rows[:, :LAT], preferred_element_type=jnp.float32
    ).astype(jnp.bfloat16)
    projected = jnp.einsum(
        "qc,dc->qd", output_latent, value_weight, preferred_element_type=jnp.float32
    )
    return jnp.where(valid_rows[:, None], projected, 0.0).astype(jnp.bfloat16)


def latent_query(head_queries, weight):
    query_latent = jnp.dot(
        head_queries[:, :HD], weight[:HD], preferred_element_type=jnp.float32
    ).astype(jnp.bfloat16)
    return jnp.concatenate([query_latent, head_queries[:, HD:]], axis=-1)


def per_device(q_heads, kv_latent, latent_gain, kv_up, offsets, lengths, block_order, owners):
    groups = lax.axis_size("ctx")
    context = lax.axis_index("ctx")
    local_rows = q_heads.shape[1]
    block_width = local_rows // 2
    segment_length = local_rows * groups
    heads_here = kv_up.shape[0]
    order_row = block_order[0]
    length_here = lengths[0]
    row_index = jnp.arange(local_rows, dtype=jnp.int32)
    blocks_here = lax.dynamic_slice_in_dim(order_row, 2 * context, 2)
    positions = blocks_here[row_index // block_width] * block_width + row_index % block_width
    angles = angle_table(offsets[0] + positions, ROPE)
    cache_rows = make_cache(kv_latent[0], latent_gain, angles)
    key_rows = lax.all_gather(cache_rows, "ctx", axis=0, tiled=True)
    query_parts = q_heads[0].reshape(local_rows, HEADS, HD + ROPE)
    query_rope = rotate(query_parts[:, :, HD:].astype(jnp.float32), angles[:, None, :]).astype(
        jnp.bfloat16
    )
    joined = jnp.concatenate([query_parts[:, :, :HD], query_rope], axis=-1)
    outgoing = joined.reshape(local_rows, groups, heads_here * (HD + ROPE))
    incoming = lax.all_to_all(outgoing, "ctx", split_axis=1, concat_axis=0, tiled=True)
    block_ids = jnp.arange(2 * groups, dtype=jnp.int32)
    inverse = jnp.sum(
        jnp.where(order_row[None, :] == block_ids[:, None], block_ids[None, :], 0), axis=1
    )
    sorted_queries = jnp.take(
        incoming.reshape(2 * groups, block_width, heads_here, HD + ROPE), inverse, axis=0
    )
    sorted_queries = sorted_queries.reshape(segment_length, heads_here, HD + ROPE)
    sorted_keys = jnp.take(
        key_rows.reshape(2 * groups, block_width, key_rows.shape[1]), inverse, axis=0
    )
    sorted_keys = sorted_keys.reshape(segment_length, key_rows.shape[1])
    sorted_positions = jnp.arange(segment_length, dtype=jnp.int32)
    tile_rows = min(256, segment_length)

    def one_head(head_index):
        weight = kv_up[head_index]
        head_queries = lax.dynamic_index_in_dim(sorted_queries, head_index, 1, keepdims=False)
        queries = latent_query(head_queries, weight)
        pieces = []
        for tile_index in range(segment_length // tile_rows):
            lower_row = tile_index * tile_rows
            upper_row = lower_row + tile_rows
            query_pos = sorted_positions[lower_row:upper_row]
            key_pos = sorted_positions[:upper_row]
            allowed = (key_pos[None, :] <= query_pos[:, None]) & (key_pos[None, :] < length_here)
            pieces.append(
                attend(
                    queries[lower_row:upper_row],
                    sorted_keys[:upper_row],
                    weight[HD:],
                    allowed,
                    query_pos < length_here,
                )
            )
        return jnp.concatenate(pieces, axis=0)

    per_head = lax.map(one_head, jnp.arange(heads_here, dtype=jnp.int32))
    merged = per_head.transpose(1, 0, 2).reshape(2 * groups, block_width, heads_here * HD)
    device_order = jnp.take(merged, order_row, axis=0).reshape(segment_length, 1, heads_here * HD)
    returned = lax.all_to_all(
        as_sent(device_order), "ctx", split_axis=0, concat_axis=1, tiled=True
    ).astype(device_order.dtype)
    attn_out = returned.reshape(1, local_rows, HEADS * HD)
    page_rows = cache_rows.reshape(2, block_width * cache_rows.shape[1])
    owner_here = lax.axis_index("req")
    everyone = lax.all_gather(page_rows, "req", axis=0, tiled=True)
    named_owner = owners.reshape(-1)
    source_index = jnp.arange(named_owner.shape[0], dtype=jnp.int32)
    matches = named_owner == owner_here
    first_slot = jnp.min(jnp.where(matches, source_index, named_owner.shape[0]))
    second_slot = jnp.min(
        jnp.where(matches & (source_index != first_slot), source_index, named_owner.shape[0])
    )
    picked = jnp.take(everyone, jnp.stack([first_slot, second_slot]), axis=0)
    shipped = picked.reshape(1, 2, page_rows.shape[1])
    return (attn_out, shipped)


def solution(mesh):
    in_specs = (
        P("req", "ctx", None),
        P("req", "ctx", None),
        P(),
        P("ctx", None, None),
        P("req"),
        P("req"),
        P("req", None),
        P(None, "ctx"),
    )
    out_specs = (P("req", "ctx", None), P("req", "ctx", None))
    return jax.shard_map(
        per_device, mesh=mesh, in_specs=in_specs, out_specs=out_specs, check_vma=False
    )
```

profile of v0, /device:TPU:0, one launch (start us, length us, event | category | flops | bytes accessed | tf_op | source)
XLA Modules:
  0.0 402.4 jit_solution(12899734093202087827)
XLA Ops:
  7.2 3.5 copy.53
  20.3 4.4 %all-to-all-start = ((bf16[128,2,6144]{0,2,1:T(8,128)(2,1)}), bf16[128,2,6144]{0,2,1:T(8,128)(2,1)S(1)}, u32[]{:S(2)}, u32[]{:S(2)}) async-start(bf16[128,2,6144]{0,2,1:T(8,128)(2,1)} %bitcast.80), calls=%async_computation | async-start | bytes 6291456 | tf_op jit(solution)/shard_map/all_to_all | solution.py:100
  26.3 38.9 %all_gather.6 = bf16[256,576]{0,1:T(8,128)(2,1)} all-gather(bf16[128,576]{0,1:T(8,128)(2,1)S(1)} %pad_maximum_fusion.1), channel_id=1, replica_groups=mesh['req'=16,'ctx'=2] {'ctx'}, dimensions={0}, use_global_device_ids=true | all-gather | bytes 442368 | tf_op jit(solution)/shard_map/all_gather | solution.py:93
  70.6 3.2 copy.54
  73.9 5.8 %reshape.376 = bf16[4,64,32,192]{3,2,1,0:T(8,128)(2,1)} reshape(bf16[2,128,1,6144]{3,1,0,2:T(8,128)(2,1)S(1)} %copy.54) | data formatting | bytes 6291456 | tf_op jit(solution)/shard_map/reshape | solution.py:106
  79.7 5.0 %gather_fusion = bf16[4,64,32,192]{3,2,1,0:T(8,128)(2,1)} fusion(bf16[4,64,32,192]{3,2,1,0:T(8,128)(2,1)} %reshape.376, s32[1024]{0:T(1024)S(1)} %pad_clamp_fusion.2), kind=kCustom, calls=%fused_computation | custom fusion | bytes 6291472 | tf_op jit(solution)/shard_map/jit(_take)/gather | solution.py:105
  84.6 6.5 %copy.55 = bf16[256,32,192]{0,2,1:T(8,128)(2,1)S(1)} copy(bf16[256,32,192]{2,1,0:T(8,128)(2,1)} %bitcast.78) | data formatting | bytes 6291456 | tf_op jit(solution)/shard_map/jit(_take)/gather | solution.py:105
  93.1 236.9 %while.12 = (s32[]{:T(128)}, bf16[32,256,128]{2,1,0:T(8,128)(2,1)}, s32[]{:T(128)}, s32[32]{0:T(128)S(1)}, bf16[256,32,192]{0,2,1:T(8,128)(2,1)}, /*index=5*/bf1...) while((s32[]{:T(128)}, bf16[32,256,128]{2,1,0:T(8,128)(2,1)}, ...), condition=%wide.region_5.6_spmd.clone.clone, body=%wide.region_2.5_spmd.clone.clone.sunk | while | flops 211287808 | bytes 2628283 | solution.py:138
  172.5 2.0 fusion.49
  202.2 2.0 fusion.49
  231.8 2.0 fusion.49
  313.2 2.0 fusion.49
  330.0 4.3 %copy.57 = bf16[256,32,128]{2,1,0:T(8,128)(2,1)} copy(bf16[256,32,128]{2,0,1:T(8,128)(2,1)} %bitcast.85) | data formatting | bytes 4194304 | tf_op jit(solution)/shard_map/transpose | solution.py:139
  334.3 2.8 reshape.378
  337.1 2.0 gather_fusion.2
  341.5 3.0 reduce.2
  344.5 3.8 reshape.440
  348.3 4.1 %all-to-all-start.1 = ((bf16[2,2,262144]{2,1,0:T(2,128)(2,1)}), bf16[2,2,262144]{2,1,0:T(2,128)(2,1)S(1)}, u32[]{:S(2)}, u32[]{:S(2)}) async-start(bf16[2,2,262144]{2,1,0:T(2,128)(2,1)} %reshape.440), calls=%async_computation.1 | async-start | bytes 4194304 | tf_op jit(solution)/shard_map/all_to_all | solution.py:141
  357.0 19.9 %all-to-all-done.1 = bf16[2,2,262144]{2,1,0:T(2,128)(2,1)S(1)} async-done(((bf16[2,2,262144]{2,1,0:T(2,128)(2,1)}), bf16[2,2,262144]{2,1,0:T(2,128)(2,1)S(1)}, u32[]{:S(2)}, u32[]{:S(2)}) %all-to-all-start.1) | async-done | bytes 2097184 | tf_op jit(solution)/shard_map/all_to_all | solution.py:141
  376.9 3.1 reshape.441
  380.0 4.5 %copy.63 = bf16[256,1,4096]{2,0,1:T(8,128)(2,1)S(1)} copy(bf16[256,1,4096]{2,1,0:T(2,128)(2,1)} %reshape.441) | data formatting | bytes 4194304
  384.5 2.5 copy.59
  387.0 4.1 %copy.61 = bf16[1,128,8192]{2,1,0:T(8,128)(2,1)} copy(bf16[1,128,8192]{1,2,0:T(8,128)(2,1)} %bitcast.84) | data formatting | bytes 4194304
  391.0 2.9 reshape.438
  (342 shorter events, 202.2 us)
Async XLA Ops:
  10.7 3.1 copy-start.5
  10.7 4.4 %copy-start.2 = (bf16[1,128,576]{1,2,0:T(8,128)(2,1)S(1)}, bf16[1,128,576]{1,2,0:T(8,128)(2,1)}, u32[]{:S(2)}) copy-start(bf16[1,128,576]{1,2,0:T(8,128)(2,1)} %param.11) | copy-start | bytes 442372
  13.8 4.6 %copy-start.1 = (bf16[128,64,128]{0,2,1:T(8,128)(2,1)S(1)}, bf16[128,64,128]{0,2,1:T(8,128)(2,1)}, u32[]{:S(2)}) copy-start(bf16[128,64,128]{0,2,1:T(8,128)(2,1)} %slice.83) | copy-start | bytes 6291460
  20.3 4.5 %copy-start.4 = (f32[512]{0:T(512)S(1)}, f32[512]{0:T(512)}, u32[]{:S(2)}) copy-start(f32[512]{0:T(512)} %param.12) | copy-start | bytes 6148
  20.3 48.7 %all-to-all-start = ((bf16[128,2,6144]{0,2,1:T(8,128)(2,1)}), bf16[128,2,6144]{0,2,1:T(8,128)(2,1)S(1)}, u32[]{:S(2)}, u32[]{:S(2)}) async-start(bf16[128,2,6144]{0,2,1:T(8,128)(2,1)} %bitcast.80), calls=%async_computation | async-start | bytes 6291456 | tf_op jit(solution)/shard_map/all_to_all | solution.py:100
  24.6 366.4 %all-gather.3.cloned.1.call-start = ((), (), s32[]{:S(2)}) async-start(), calls=%async_computation.2 | async-start | bytes 2506752 | tf_op jit(solution)/shard_map/all_gather | solution.py:147
  69.0 1.7 copy-start
  348.3 4.1 %copy-start.3 = (s32[16,2]{0,1:T(2,128)S(1)}, s32[16,2]{0,1:T(2,128)}, u32[]{:S(2)}) copy-start(s32[16,2]{0,1:T(2,128)} %param.17) | copy-start | bytes 388
  348.3 28.6 %all-to-all-start.1 = ((bf16[2,2,262144]{2,1,0:T(2,128)(2,1)}), bf16[2,2,262144]{2,1,0:T(2,128)(2,1)S(1)}, u32[]{:S(2)}, u32[]{:S(2)}) async-start(bf16[2,2,262144]{2,1,0:T(2,128)(2,1)} %reshape.440), calls=%async_computation.1 | async-start | bytes 4194304 | tf_op jit(solution)/shard_map/all_to_all | solution.py:141
Sparse Core Ops, SparseCore 0:
  28.3 45.2 all-gather.2
where the time goes:
time: 407 us; the launch traced here: 402 us
  local copies, waits for them, and re-layouts  113 us (28%)
  matrix products  110 us (27%)
  loops' own time  53.3 us (13%)
  other arithmetic  43.8 us (11%)
  blocking collectives  38.9 us (10%)
  waiting for transfers between devices  19.9 us (5%)
  between operations  14.9 us (4%)
  starting transfers between devices  8.44 us (2%)
    dot_general x32, matrix products, attend(): jnp.einsum('qc,dc->qd', output_latent, value_weight, preferred_element_ty...  63.2 us
    another operation x1, loops' own time, per_device(): per_head = lax.map(one_head, jnp.arange(heads_here, dtype=jnp.int32))  53.3 us
    all_gather x1, blocking collectives, per_device(): key_rows = lax.all_gather(cache_rows, 'ctx', axis=0, tiled=True)  38.9 us
    dot_general x32, matrix products, latent_query(): jnp.dot(head_queries[:, :HD], weight[:HD], preferred_element_type=jnp.flo...  36.7 us
    squeeze x32, local copies, waits for them, and re-layouts, one_head(): lax.dynamic_index_in_dim(sorted_queries, head_index, 1, keepdims=False)  28.9 us
    unnamed x19, local copies, waits for them, and re-layouts  24.4 us
    lt x32, other arithmetic, one_head(): query_pos < length_here  21 us
    all_to_all x1, waiting for transfers between devices, per_device(): lax.all_to_all(as_sent(device_order), 'ctx', split_axis=0, concat_axis=1,...  19.9 us
  transfers between devices with their start and end apart: 3, of which 1 were waited for; matrix products, arithmetic and copies ran while one was open for 62% of the time, Pallas kernels for 0%

commit v1 on v0

v1 whole, which is shorter than its diff:
```python
import functools
import math

import jax
import jax.numpy as jnp
from jax import lax
from jax.experimental import pallas as pl
from jax.experimental.pallas import tpu as pltpu
from jax.sharding import PartitionSpec as P

HEADS = 64
HD = 128
ROPE = 64
LAT = 512
QW = HD + ROPE

theta_base = 10000.0
epsilon = 1e-06
masked_fill = -1e30
MESH = pl.DeviceIdType.MESH


def row_positions(order_ref, shape, axis, block_width, blocks):
    index = lax.broadcasted_iota(jnp.int32, shape, axis)
    block = index // block_width
    position = index - block * block_width
    for j in range(blocks):
        position = position + jnp.where(block == j, order_ref[0, j] * block_width, 0)
    return position


def attention_kernel(
    groups,
    chunk_heads,
    order_ref,
    length_ref,
    q_hbm,
    cache_ref,
    cos_ref,
    sin_ref,
    w_hbm,
    out_hbm,
    qbuf,
    wbuf,
    keys,
    cache_t,
    rope_t,
    bias,
    obuf,
    w_sem,
    qown_sem,
    oown_sem,
    key_send,
    key_recv,
    q_send,
    q_recv,
    o_send,
    o_recv,
):
    me = lax.axis_index("ctx")
    rows = q_hbm.shape[0]
    segment = rows * groups
    heads = w_hbm.shape[0]
    chunks = heads // chunk_heads
    q_width = chunk_heads * QW
    o_width = chunk_heads * HD
    blocks = order_ref.shape[1]
    block_width = segment // blocks

    def peer(step):
        return lax.rem(me + step, groups)

    def own_rows(index):
        return pl.ds(pl.multiple_of(index * rows, rows), rows)

    def q_columns(group, c):
        return pl.ds(pl.multiple_of(group * (heads * QW) + c * q_width, 128), q_width)

    def o_columns(group, c):
        return pl.ds(pl.multiple_of(group * (heads * HD) + c * o_width, 128), o_width)

    def key_copy(step):
        return pltpu.make_async_remote_copy(
            src_ref=cache_ref,
            dst_ref=keys.at[own_rows(me)],
            send_sem=key_send.at[step - 1],
            recv_sem=key_recv.at[step - 1],
            device_id={"ctx": peer(step)},
            device_id_type=MESH,
        )

    def q_copy(step, c):
        return pltpu.make_async_remote_copy(
            src_ref=q_hbm.at[:, q_columns(peer(step), c)],
            dst_ref=qbuf.at[c, own_rows(me)],
            send_sem=q_send.at[step - 1, c],
            recv_sem=q_recv.at[step - 1, c],
            device_id={"ctx": peer(step)},
            device_id_type=MESH,
        )

    def o_copy(step, c):
        return pltpu.make_async_remote_copy(
            src_ref=obuf.at[c, own_rows(peer(step))],
            dst_ref=out_hbm.at[:, o_columns(me, c)],
            send_sem=o_send.at[step - 1, c],
            recv_sem=o_recv.at[step - 1, c],
            device_id={"ctx": peer(step)},
            device_id_type=MESH,
        )

    def q_own(c):
        return pltpu.make_async_copy(
            q_hbm.at[:, q_columns(me, c)], qbuf.at[c, own_rows(me)], qown_sem.at[c]
        )

    def w_copy(c):
        return pltpu.make_async_copy(
            w_hbm.at[pl.ds(c * chunk_heads, chunk_heads)], wbuf.at[c], w_sem.at[c]
        )

    def o_own(c):
        return pltpu.make_async_copy(
            obuf.at[c, own_rows(me)], out_hbm.at[:, o_columns(me, c)], oown_sem.at[c]
        )

    barrier = pltpu.get_barrier_semaphore()
    for step in range(1, groups):
        pl.semaphore_signal(
            barrier, inc=1, device_id={"ctx": peer(step)}, device_id_type=MESH
        )
    pl.semaphore_wait(barrier, groups - 1)

    for step in range(1, groups):
        key_copy(step).start()
    for c in range(chunks):
        for step in range(1, groups):
            q_copy(step, c).start()
    for c in range(chunks):
        w_copy(c).start()
        q_own(c).start()

    keys[own_rows(me)] = cache_ref[...]
    length = length_ref[0]
    query_pos = row_positions(order_ref, (segment, 1), 0, block_width, blocks)
    key_pos = row_positions(order_ref, (1, segment), 1, block_width, blocks)
    bias[...] = jnp.where((key_pos <= query_pos) & (key_pos < length), 0.0, masked_fill)

    for step in range(1, groups):
        key_copy(step).wait()
    for g in range(groups):
        span = slice(g * rows, (g + 1) * rows)
        cache_t[:, span] = keys[span, :LAT].astype(jnp.float32).T.astype(jnp.bfloat16)
        turned = keys[span, LAT:].astype(jnp.float32)
        empty = jnp.zeros_like(turned)
        rope_t[0, :, span] = jnp.concatenate([turned, empty], axis=1).T.astype(jnp.bfloat16)
        rope_t[1, :, span] = jnp.concatenate([empty, turned], axis=1).T.astype(jnp.bfloat16)

    scale = (QW ** -0.5) * math.log2(math.e)
    tile = min(256, segment)
    lane = lax.broadcasted_iota(jnp.int32, (tile, 128), 1)
    low = lane < ROPE
    first = (lane & (ROPE // 2)) == 0

    def one_chunk(c, carry):
        w_copy(c).wait()
        q_own(c).wait()
        for step in range(1, groups):
            q_copy(step, c).wait()
        weights = wbuf[c].reshape(chunk_heads * 2 * HD, LAT)
        expanded = jnp.dot(
            weights, cache_t[...], preferred_element_type=jnp.float32
        ).astype(jnp.bfloat16)
        ones = jnp.ones((HD, segment), jnp.bfloat16)
        for t in range(segment // tile):
            span = slice(t * tile, (t + 1) * tile)
            valid = (
                row_positions(order_ref, (tile, HD), 0, block_width, blocks)
                if segment == tile
                else None
            )
            if valid is None:
                index = lax.broadcasted_iota(jnp.int32, (tile, HD), 0) + t * tile
                block = index // block_width
                valid = index - block * block_width
                for j in range(blocks):
                    valid = valid + jnp.where(block == j, order_ref[0, j] * block_width, 0)
            valid = valid < length
            for pair in range(chunk_heads // 2):
                at = pair * 2 * QW
                part0 = qbuf[c, span, at : at + 128]
                part1 = qbuf[c, span, at + 128 : at + 256].astype(jnp.float32)
                part2 = qbuf[c, span, at + 256 : at + 384].astype(jnp.float32)
                plain = jnp.where(low, part1, part2)
                other = jnp.where(
                    first,
                    pltpu.roll(plain, 128 - ROPE // 2, 1),
                    pltpu.roll(plain, ROPE // 2, 1),
                )
                turned = (plain * cos_ref[span] + other * sin_ref[span]).astype(jnp.bfloat16)
                swapped = jnp.where(low, part2, part1).astype(jnp.bfloat16)
                for odd in range(2):
                    top = (pair * 2 + odd) * 2 * HD
                    key_t = expanded[top : top + HD]
                    value_t = expanded[top + HD : top + 2 * HD]
                    if odd:
                        key_t = jnp.concatenate(
                            [key_t[HD // 2 :], key_t[: HD // 2], rope_t[1]], axis=0
                        )
                        query = jnp.concatenate([swapped, turned], axis=1)
                    else:
                        key_t = jnp.concatenate([key_t, rope_t[0]], axis=0)
                        query = jnp.concatenate([part0, turned], axis=1)
                    scores = (
                        jnp.dot(query, key_t, preferred_element_type=jnp.float32) * scale
                        + bias[span]
                    )
                    top_score = jnp.max(scores, axis=-1, keepdims=True)
                    weight = jnp.exp2(scores - top_score).astype(jnp.bfloat16)
                    summed = lax.dot_general(
                        weight,
                        jnp.concatenate([value_t, ones], axis=0),
                        (((1,), (1,)), ((), ())),
                        preferred_element_type=jnp.float32,
                    )
                    result = jnp.where(valid, summed[:, :HD] / summed[:, HD:], 0.0)
                    column = (pair * 2 + odd) * HD
                    obuf[c, span, column : column + HD] = result.astype(jnp.bfloat16)
        for step in range(1, groups):
            o_copy(step, c).start()
        o_own(c).start()
        return carry

    lax.fori_loop(0, chunks, one_chunk, 0)

    def finish(c, carry):
        o_own(c).wait()
        for step in range(1, groups):
            o_copy(step, c).wait()
        return carry

    lax.fori_loop(0, chunks, finish, 0)


def attention(q, cache_rows, cosine, sine, kv_up, order, length):
    groups = lax.axis_size("ctx")
    rows = q.shape[0]
    segment = rows * groups
    heads = kv_up.shape[0]
    chunk_heads = min(4, heads)
    chunks = heads // chunk_heads
    in_vmem = pl.BlockSpec(memory_space=pltpu.VMEM)
    in_smem = pl.BlockSpec(memory_space=pltpu.SMEM)
    anywhere = pl.BlockSpec(memory_space=pl.ANY)
    dma = pltpu.SemaphoreType.DMA
    others = groups - 1
    return pl.pallas_call(
        functools.partial(attention_kernel, groups, chunk_heads),
        out_shape=jax.ShapeDtypeStruct((rows, HEADS * HD), jnp.bfloat16),
        in_specs=[in_smem, in_smem, anywhere, in_vmem, in_vmem, in_vmem, anywhere],
        out_specs=anywhere,
        scratch_shapes=[
            pltpu.VMEM((chunks, segment, chunk_heads * QW), jnp.bfloat16),
            pltpu.VMEM((chunks, chunk_heads, 2 * HD, LAT), jnp.bfloat16),
            pltpu.VMEM((segment, LAT + ROPE), jnp.bfloat16),
            pltpu.VMEM((LAT, segment), jnp.bfloat16),
            pltpu.VMEM((2, 2 * ROPE, segment), jnp.bfloat16),
            pltpu.VMEM((segment, segment), jnp.float32),
            pltpu.VMEM((chunks, segment, chunk_heads * HD), jnp.bfloat16),
            dma((chunks,)),
            dma((chunks,)),
            dma((chunks,)),
            dma((others,)),
            dma((others,)),
            dma((others, chunks)),
            dma((others, chunks)),
            dma((others, chunks)),
            dma((others, chunks)),
        ],
        compiler_params=pltpu.CompilerParams(
            collective_id=0, has_side_effects=True, vmem_limit_bytes=52 * 2**20
        ),
        cost_estimate=pl.CostEstimate(
            flops=2 * heads * segment * (2 * HD * LAT + 4 * HD * segment),
            bytes_accessed=2 * (2 * rows * HEADS * QW + heads * 2 * HD * LAT + rows * HEADS * HD),
            transcendentals=heads * segment * segment,
        ),
    )(order, length, q, cache_rows, cosine, sine, kv_up)


def per_device(q_heads, kv_latent, latent_gain, kv_up, offsets, lengths, block_order, owners):
    groups = lax.axis_size("ctx")
    context = lax.axis_index("ctx")
    local_rows = q_heads.shape[1]
    segment = local_rows * groups
    blocks = block_order.shape[1]
    block_width = segment // blocks
    order_row = block_order[0]
    positions = (
        order_row[:, None] * block_width + jnp.arange(block_width, dtype=jnp.int32)[None, :]
    ).reshape(segment)
    half = ROPE // 2
    frequency = jnp.exp(-math.log(theta_base) * jnp.arange(half, dtype=jnp.float32) / half)
    angles = (offsets[0] + positions).astype(jnp.float32)[:, None] * frequency[None, :]
    cosine = jnp.cos(angles)
    sine = jnp.sin(angles)
    latent_rows = kv_latent[0]
    latent = latent_rows[:, :LAT].astype(jnp.float32)
    mean_square = jnp.mean(latent * latent, axis=-1, keepdims=True)
    normed = (latent * lax.rsqrt(mean_square + epsilon) * latent_gain).astype(jnp.bfloat16)
    cos_here = lax.dynamic_slice_in_dim(cosine, context * local_rows, local_rows)
    sin_here = lax.dynamic_slice_in_dim(sine, context * local_rows, local_rows)
    first = latent_rows[:, LAT : LAT + half].astype(jnp.float32)
    second = latent_rows[:, LAT + half :].astype(jnp.float32)
    key_rope = jnp.concatenate(
        [first * cos_here - second * sin_here, second * cos_here + first * sin_here], axis=-1
    ).astype(jnp.bfloat16)
    cache_rows = jnp.concatenate([normed, key_rope], axis=-1)

    page_rows = cache_rows.reshape(local_rows // block_width, block_width * cache_rows.shape[1])
    everyone = lax.all_gather(page_rows, "req", axis=0, tiled=True)

    attn_out = attention(
        q_heads[0],
        cache_rows,
        jnp.concatenate([cosine] * 4, axis=1),
        jnp.concatenate([-sine, sine, -sine, sine], axis=1),
        kv_up,
        block_order,
        lengths,
    )

    owner_here = lax.axis_index("req")
    named_owner = owners.reshape(-1)
    source_index = jnp.arange(named_owner.shape[0], dtype=jnp.int32)
    matches = named_owner == owner_here
    first_slot = jnp.min(jnp.where(matches, source_index, named_owner.shape[0]))
    second_slot = jnp.max(jnp.where(matches, source_index, -1))
    shipped = jnp.concatenate(
        [
            lax.dynamic_slice_in_dim(everyone, first_slot, 1),
            lax.dynamic_slice_in_dim(everyone, second_slot, 1),
        ],
        axis=0,
    )
    return (attn_out[None], shipped[None])


def solution(mesh):
    in_specs = (
        P("req", "ctx", None),
        P("req", "ctx", None),
        P(),
        P("ctx", None, None),
        P("req"),
        P("req"),
        P("req", None),
        P(None, "ctx"),
    )
    out_specs = (P("req", "ctx", None), P("req", "ctx", None))
    return jax.shard_map(
        per_device, mesh=mesh, in_specs=in_specs, out_specs=out_specs, check_vma=False
    )
```

time: 407 us -> 97.8 us (0.24); the launches traced: 402 us -> 97.4 us
  matrix products: 110 us -> 0 us
  local copies, waits for them, and re-layouts: 113 us -> 8.32 us
  Pallas kernels: 0 us -> 64.6 us
  loops' own time: 53.3 us -> 0 us
  blocking collectives: 38.9 us -> 0 us
  other arithmetic: 43.8 us -> 5.04 us
  waiting for transfers between devices: 19.9 us -> 0.04 us
  starting transfers between devices: 8.44 us -> 0.04 us
  between operations: 14.9 us -> 19.4 us
    dot_general x96 -> x0, matrix products: 110 us -> none  [the longest x32 63.2 us: attend(): jnp.einsum('qc,dc->qd', output_latent, value_weight, preferred_element_ty...]
    pallas_call x0 -> x1, Pallas kernels: none -> 64.6 us  [attention(): pl.pallas_call(functools.partial(attention_kernel, groups, chunk_heads),...]
    another operation x1 -> x0, loops' own time: 53.3 us -> none  [per_device(): per_head = lax.map(one_head, jnp.arange(heads_here, dtype=jnp.int32))]
    all_gather x1 -> x0, blocking collectives: 38.9 us -> none  [per_device(): key_rows = lax.all_gather(cache_rows, 'ctx', axis=0, tiled=True)]
    squeeze x32 -> x0, local copies, waits for them, and re-layouts: 28.9 us -> none  [one_head(): lax.dynamic_index_in_dim(sorted_queries, head_index, 1, keepdims=False)]
    lt x32 -> x0, other arithmetic: 21 us -> none  [one_head(): query_pos < length_here]
    all_to_all x2 -> x0, waiting for transfers between devices: 19.9 us -> none  [the longest x1 19.9 us: per_device(): lax.all_to_all(as_sent(device_order), 'ctx', split_axis=0, concat_axis=1,...]
    dynamic_slice x33 -> x1, local copies, waits for them, and re-layouts: 17.6 us -> 0.32 us  [per_device(): lax.dynamic_slice_in_dim(everyone, first_slot, 1)]
  transfers between devices with their start and end apart: 3 -> 1, of which waited for: 1 -> 0; matrix products, arithmetic and copies ran while one was open for 62% -> 2% of each run, Pallas kernels for 0% -> 66%
where the time goes in v1:
time: 97.8 us; the launch traced here: 97.4 us
  Pallas kernels  64.6 us (66%)
  between operations  19.4 us (20%)
  local copies, waits for them, and re-layouts  8.32 us (9%)
  other arithmetic  5.04 us (5%)
    pallas_call x1, Pallas kernels, attention(): pl.pallas_call(functools.partial(attention_kernel, groups, chunk_heads),...  64.6 us
    unnamed x6, local copies, waits for them, and re-layouts  7.92 us
  transfers between devices with their start and end apart: 1, of which 0 were waited for; matrix products, arithmetic and copies ran while one was open for 2% of the time, Pallas kernels for 66%

profile of v1, /device:TPU:0, one launch (start us, length us, event | category | flops | bytes accessed | tf_op | source)
XLA Modules:
  0.0 97.4 jit_solution(16786951583403524730)
XLA Ops:
  7.2 0.0 copy-start
  7.2 0.0 all-gather.3.cloned.1.call-start
  7.9 0.7 multiply_bitcast_fusion
  8.6 0.1 add_convert_fusion
  8.6 0.1 convert_element_type.27
  8.7 1.1 %copy.13 = bf16[1,128,576]{2,1,0:T(8,128)(2,1)S(1)} copy(bf16[1,128,576]{1,2,0:T(8,128)(2,1)} %param.9) | data formatting | bytes 294912 | tf_op args[1]
  9.8 0.1 fusion
  9.9 0.8 fusion.2
  10.7 0.5 fusion.7
  11.2 0.1 fusion.4
  11.3 0.1 pad_maximum_fusion.cache_ref
  11.4 0.9 reshape.52
  12.3 0.0 all-gather.3.cloned.1.call-update
  12.3 1.4 %select_reduce_fusion.1 = (s32[]{:T(128)}, s32[]{:T(128)}) fusion(s32[16,2]{0,1:T(2,128)} %param.15, s32[]{:T(128)S(6)} %axis_index.25), kind=kLoop, calls=%fused_computation.22 | loop fusion | flops 222 | bytes 140 | tf_op jit(solution)/shard_map/reduce_min | solution.py:337
  17.1 0.3 pad_maximum_fusion.1
  17.3 0.0 copy-done
  17.3 64.6 %shard_map.95 = bf16[128,8192]{1,0:T(8,128)(2,1)} custom-call(s32[1,4]{1,0:T(1,128)S(1)} %copy-done, s32[1]{0:T(128)S(6)} %copy.16.length_ref, bf16[128,12288]{1,0:T(8,128)(2,1)} %bitcast.13, bf16[128,576]{1,0:T(8,128)(2,1)S(1)} %pad_maximum_fusion.cache_ref, f32[256,128]{1,0:T(8,128)S(1)} %get-tuple-element.11.cos_ref, ...), custom_call_target="tpu_custom_call" | custom-call | flops 4294967296 | bytes 16777216 | tf_op jit(solution)/shard_map/pallas_call | solution.py:257
  83.2 0.0 all-gather.3.cloned.1.call-done
  83.3 2.9 %reshape.53 = bf16[32,36864]{1,0:T(8,128)(2,1)S(1)} reshape(bf16[16,2,36864]{2,1,0:T(2,128)(2,1)} %all-gather.3.cloned.1.call-done) | data formatting | bytes 4718592
  86.2 0.3 constant_dynamic-slice_fusion.1
  86.5 1.0 %maximum_bitcast_fusion = bf16[1,2,36864]{2,1,0:T(2,128)(2,1)} fusion(bf16[1,36864]{1,0:T(2,128)(2,1)S(1)} %get-tuple-element.5, bf16[1,36864]{1,0:T(2,128)(2,1)S(1)} %get-tuple-element.4), kind=kLoop, calls=%fused_computation.8 | loop fusion | flops 294912 | bytes 294912 | tf_op jit(solution)/shard_map/broadcast_in_dim | solution.py:346
  87.5 3.1 %copy.17 = bf16[1,128,8192]{2,1,0:T(8,128)(2,1)} copy(bf16[1,128,8192]{2,1,0:T(8,128)(2,1)} %bitcast.9) | data formatting | bytes 4194304
  (2 shorter events, 0.0 us)
Async XLA Ops:
  7.2 10.2 %copy-start = (s32[1,4]{1,0:T(1,128)S(1)}, s32[1,4]{1,0:T(1,128)}, u32[]{:S(2)}) copy-start(s32[1,4]{1,0:T(1,128)} %order_ref.1) | copy-start | bytes 52
  7.2 76.1 %all-gather.3.cloned.1.call-start = ((), (), s32[]{:S(2)}) async-start(), calls=%async_computation | async-start | bytes 2506752 | tf_op jit(solution)/shard_map/all_gather | solution.py:321
Sparse Core Ops, SparseCore 0:
  12.4 45.0 all-gather.2

commit v2 on v1

--- a/solution.py
+++ b/solution.py
@@ -3,6 +3,7 @@
 
 import jax
 import jax.numpy as jnp
+import numpy as np
 from jax import lax
 from jax.experimental import pallas as pl
 from jax.experimental.pallas import tpu as pltpu
@@ -31,18 +32,26 @@
 
 def attention_kernel(
     groups,
+    lines,
     chunk_heads,
     order_ref,
+    offset_ref,
     length_ref,
+    owners_ref,
+    gain_ref,
+    frequency_ref,
+    kv_ref,
     q_hbm,
-    cache_ref,
+    w_hbm,
+    out_hbm,
+    shipped_ref,
+    qbuf,
+    wbuf,
+    raw,
+    keys,
+    pages,
     cos_ref,
     sin_ref,
-    w_hbm,
-    out_hbm,
-    qbuf,
-    wbuf,
-    keys,
     cache_t,
     rope_t,
     bias,
@@ -56,8 +65,19 @@
     q_recv,
     o_send,
     o_recv,
+    line_send,
+    line_recv,
+    side_send,
+    side_recv,
+    core_send,
+    core_recv,
 ):
     me = lax.axis_index("ctx")
+    request = lax.axis_index("req")
+    along, across = lines
+    core = lax.rem(request, 2)
+    side = lax.rem(request // 2, across)
+    line = request // (2 * across)
     rows = q_hbm.shape[0]
     segment = rows * groups
     heads = w_hbm.shape[0]
@@ -67,6 +87,51 @@
     blocks = order_ref.shape[1]
     block_width = segment // blocks
 
+    def device(line_at, side_at, core_at):
+        return {"req": (line_at * across + side_at) * 2 + core_at}
+
+    def line_peer(step):
+        return device(lax.rem(line + step, along), side, core)
+
+    def side_peer(step):
+        return device(line, lax.rem(side + step, across), core)
+
+    def core_peer():
+        return device(line, side, 1 - core)
+
+    def line_copy(step):
+        piece = pages.at[pl.ds((core * across + side) * along + line, 1)]
+        return pltpu.make_async_remote_copy(
+            src_ref=piece,
+            dst_ref=piece,
+            send_sem=line_send.at[step - 1],
+            recv_sem=line_recv.at[step - 1],
+            device_id=line_peer(step),
+            device_id_type=MESH,
+        )
+
+    def side_copy(step):
+        piece = pages.at[pl.ds((core * across + side) * along, along)]
+        return pltpu.make_async_remote_copy(
+            src_ref=piece,
+            dst_ref=piece,
+            send_sem=side_send.at[step - 1],
+            recv_sem=side_recv.at[step - 1],
+            device_id=side_peer(step),
+            device_id_type=MESH,
+        )
+
+    def core_copy():
+        piece = pages.at[pl.ds(core * (across * along), across * along)]
+        return pltpu.make_async_remote_copy(
+            src_ref=piece,
+            dst_ref=piece,
+            send_sem=core_send.at[0],
+            recv_sem=core_recv.at[0],
+            device_id=core_peer(),
+            device_id_type=MESH,
+        )
+
     def peer(step):
         return lax.rem(me + step, groups)
 
@@ -81,8 +146,8 @@
 
     def key_copy(step):
         return pltpu.make_async_remote_copy(
-            src_ref=cache_ref,
-            dst_ref=keys.at[own_rows(me)],
+            src_ref=kv_ref,
+            dst_ref=raw.at[own_rows(me)],
             send_sem=key_send.at[step - 1],
             recv_sem=key_recv.at[step - 1],
             device_id={"ctx": peer(step)},
@@ -129,7 +194,12 @@
         pl.semaphore_signal(
             barrier, inc=1, device_id={"ctx": peer(step)}, device_id_type=MESH
         )
-    pl.semaphore_wait(barrier, groups - 1)
+    for step in range(1, along):
+        pl.semaphore_signal(barrier, inc=1, device_id=line_peer(step), device_id_type=MESH)
+    for step in range(1, across):
+        pl.semaphore_signal(barrier, inc=1, device_id=side_peer(step), device_id_type=MESH)
+    pl.semaphore_signal(barrier, inc=1, device_id=core_peer(), device_id_type=MESH)
+    pl.semaphore_wait(barrier, groups + along + across - 2)
 
     for step in range(1, groups):
         key_copy(step).start()
@@ -140,14 +210,39 @@
         w_copy(c).start()
         q_own(c).start()
 
-    keys[own_rows(me)] = cache_ref[...]
     length = length_ref[0]
+    row_pos = row_positions(order_ref, (segment, HD), 0, block_width, blocks)
+    angles = (row_pos + offset_ref[0]).astype(jnp.float32) * frequency_ref[...]
+    wide_lane = lax.broadcasted_iota(jnp.int32, (segment, HD), 1)
+    cos_ref[...] = jnp.cos(angles)
+    sine = jnp.sin(angles)
+    sin_ref[...] = jnp.where((wide_lane & (ROPE // 2)) == 0, -sine, sine)
+
+    def normalise(group):
+        latent = raw[own_rows(group), :LAT].astype(jnp.float32)
+        mean_square = jnp.mean(latent * latent, axis=-1, keepdims=True)
+        normed = latent * lax.rsqrt(mean_square + epsilon) * gain_ref[...]
+        keys[own_rows(group), :LAT] = normed.astype(jnp.bfloat16)
+        tail = raw[own_rows(group), LAT:].astype(jnp.float32)
+        crossed = jnp.concatenate([tail[:, ROPE // 2 :], tail[:, : ROPE // 2]], axis=1)
+        turned = (
+            tail * cos_ref[own_rows(group), :ROPE] + crossed * sin_ref[own_rows(group), :ROPE]
+        )
+        keys[own_rows(group), LAT:] = turned.astype(jnp.bfloat16)
+
+    raw[own_rows(me)] = kv_ref[...]
+    normalise(me)
+    pages[(core * across + side) * along + line] = keys[own_rows(me)]
+    for step in range(1, along):
+        line_copy(step).start()
+
     query_pos = row_positions(order_ref, (segment, 1), 0, block_width, blocks)
     key_pos = row_positions(order_ref, (1, segment), 1, block_width, blocks)
     bias[...] = jnp.where((key_pos <= query_pos) & (key_pos < length), 0.0, masked_fill)
 
     for step in range(1, groups):
         key_copy(step).wait()
+        normalise(peer(step))
     for g in range(groups):
         span = slice(g * rows, (g + 1) * rows)
         cache_t[:, span] = keys[span, :LAT].astype(jnp.float32).T.astype(jnp.bfloat16)
@@ -163,6 +258,19 @@
     first = (lane & (ROPE // 2)) == 0
 
     def one_chunk(c, carry):
+        @pl.when(c == chunks // 4)
+        def _():
+            for step in range(1, along):
+                line_copy(step).wait()
+            for step in range(1, across):
+                side_copy(step).start()
+
+        @pl.when(c == chunks * 3 // 4)
+        def _():
+            for step in range(1, across):
+                side_copy(step).wait()
+            core_copy().start()
+
         w_copy(c).wait()
         q_own(c).wait()
         for step in range(1, groups):
@@ -174,17 +282,11 @@
         ones = jnp.ones((HD, segment), jnp.bfloat16)
         for t in range(segment // tile):
             span = slice(t * tile, (t + 1) * tile)
-            valid = (
-                row_positions(order_ref, (tile, HD), 0, block_width, blocks)
-                if segment == tile
-                else None
-            )
-            if valid is None:
-                index = lax.broadcasted_iota(jnp.int32, (tile, HD), 0) + t * tile
-                block = index // block_width
-                valid = index - block * block_width
-                for j in range(blocks):
-                    valid = valid + jnp.where(block == j, order_ref[0, j] * block_width, 0)
+            index = lax.broadcasted_iota(jnp.int32, (tile, HD), 0) + t * tile
+            block = index // block_width
+            valid = index - block * block_width
+            for j in range(blocks):
+                valid = valid + jnp.where(block == j, order_ref[0, j] * block_width, 0)
             valid = valid < length
             for pair in range(chunk_heads // 2):
                 at = pair * 2 * QW
@@ -233,6 +335,20 @@
 
     lax.fori_loop(0, chunks, one_chunk, 0)
 
+    core_copy().wait()
+    count = 0
+    picked = [jnp.zeros((block_width, keys.shape[1]), jnp.bfloat16) for _ in range(2)]
+    for source in range(2 * across * along):
+        slot = ((source % 2) * across + source // 2 % across) * along + source // (2 * across)
+        for page in range(2):
+            match = owners_ref[source, page] == request
+            content = pages[slot, page * block_width : (page + 1) * block_width]
+            for place in range(2):
+                picked[place] = jnp.where(match & (count == place), content, picked[place])
+            count = count + match.astype(jnp.int32)
+    for place in range(2):
+        shipped_ref[place] = picked[place]
+
     def finish(c, carry):
         o_own(c).wait()
         for step in range(1, groups):
@@ -242,27 +358,45 @@
     lax.fori_loop(0, chunks, finish, 0)
 
 
-def attention(q, cache_rows, cosine, sine, kv_up, order, length):
+def attention(q, kv, gain, kv_up, order, offset, length, owners):
     groups = lax.axis_size("ctx")
+    requests = lax.axis_size("req")
+    chips = requests // 2
+    along = max(d for d in range(1, chips + 1) if chips % d == 0 and d * d <= 2 * chips)
+    across = chips // along
     rows = q.shape[0]
     segment = rows * groups
+    blocks = order.shape[1]
+    block_width = segment // blocks
     heads = kv_up.shape[0]
     chunk_heads = min(4, heads)
     chunks = heads // chunk_heads
+    half = ROPE // 2
+    frequency = np.exp(
+        np.float32(-math.log(theta_base)) * np.arange(half, dtype=np.float32) / np.float32(half)
+    )
+    frequency = np.tile(frequency.astype(np.float32), 2 * HD // ROPE)[None]
     in_vmem = pl.BlockSpec(memory_space=pltpu.VMEM)
     in_smem = pl.BlockSpec(memory_space=pltpu.SMEM)
     anywhere = pl.BlockSpec(memory_space=pl.ANY)
     dma = pltpu.SemaphoreType.DMA
     others = groups - 1
     return pl.pallas_call(
-        functools.partial(attention_kernel, groups, chunk_heads),
-        out_shape=jax.ShapeDtypeStruct((rows, HEADS * HD), jnp.bfloat16),
-        in_specs=[in_smem, in_smem, anywhere, in_vmem, in_vmem, in_vmem, anywhere],
-        out_specs=anywhere,
+        functools.partial(attention_kernel, groups, (along, across), chunk_heads),
+        out_shape=(
+            jax.ShapeDtypeStruct((rows, HEADS * HD), jnp.bfloat16),
+            jax.ShapeDtypeStruct((2, block_width, LAT + ROPE), jnp.bfloat16),
+        ),
+        in_specs=[in_smem] * 4 + [in_vmem] * 3 + [anywhere] * 2,
+        out_specs=(anywhere, in_vmem),
         scratch_shapes=[
             pltpu.VMEM((chunks, segment, chunk_heads * QW), jnp.bfloat16),
             pltpu.VMEM((chunks, chunk_heads, 2 * HD, LAT), jnp.bfloat16),
             pltpu.VMEM((segment, LAT + ROPE), jnp.bfloat16),
+            pltpu.VMEM((segment, LAT + ROPE), jnp.bfloat16),
+            pltpu.VMEM((requests, rows, LAT + ROPE), jnp.bfloat16),
+            pltpu.VMEM((segment, HD), jnp.float32),
+            pltpu.VMEM((segment, HD), jnp.float32),
             pltpu.VMEM((LAT, segment), jnp.bfloat16),
             pltpu.VMEM((2, 2 * ROPE, segment), jnp.bfloat16),
             pltpu.VMEM((segment, segment), jnp.float32),
@@ -276,74 +410,36 @@
             dma((others, chunks)),
             dma((others, chunks)),
             dma((others, chunks)),
+            dma((along - 1,)),
+            dma((along - 1,)),
+            dma((across - 1,)),
+            dma((across - 1,)),
+            dma((1,)),
+            dma((1,)),
         ],
         compiler_params=pltpu.CompilerParams(
-            collective_id=0, has_side_effects=True, vmem_limit_bytes=52 * 2**20
+            collective_id=0, has_side_effects=True, vmem_limit_bytes=56 * 2**20
         ),
         cost_estimate=pl.CostEstimate(
             flops=2 * heads * segment * (2 * HD * LAT + 4 * HD * segment),
             bytes_accessed=2 * (2 * rows * HEADS * QW + heads * 2 * HD * LAT + rows * HEADS * HD),
             transcendentals=heads * segment * segment,
         ),
-    )(order, length, q, cache_rows, cosine, sine, kv_up)
+    )(order, offset, length, owners, gain, jnp.asarray(frequency), kv, q, kv_up)
 
 
 def per_device(q_heads, kv_latent, latent_gain, kv_up, offsets, lengths, block_order, owners):
-    groups = lax.axis_size("ctx")
-    context = lax.axis_index("ctx")
-    local_rows = q_heads.shape[1]
-    segment = local_rows * groups
-    blocks = block_order.shape[1]
-    block_width = segment // blocks
-    order_row = block_order[0]
-    positions = (
-        order_row[:, None] * block_width + jnp.arange(block_width, dtype=jnp.int32)[None, :]
-    ).reshape(segment)
-    half = ROPE // 2
-    frequency = jnp.exp(-math.log(theta_base) * jnp.arange(half, dtype=jnp.float32) / half)
-    angles = (offsets[0] + positions).astype(jnp.float32)[:, None] * frequency[None, :]
-    cosine = jnp.cos(angles)
-    sine = jnp.sin(angles)
-    latent_rows = kv_latent[0]
-    latent = latent_rows[:, :LAT].astype(jnp.float32)
-    mean_square = jnp.mean(latent * latent, axis=-1, keepdims=True)
-    normed = (latent * lax.rsqrt(mean_square + epsilon) * latent_gain).astype(jnp.bfloat16)
-    cos_here = lax.dynamic_slice_in_dim(cosine, context * local_rows, local_rows)
-    sin_here = lax.dynamic_slice_in_dim(sine, context * local_rows, local_rows)
-    first = latent_rows[:, LAT : LAT + half].astype(jnp.float32)
-    second = latent_rows[:, LAT + half :].astype(jnp.float32)
-    key_rope = jnp.concatenate(
-        [first * cos_here - second * sin_here, second * cos_here + first * sin_here], axis=-1
-    ).astype(jnp.bfloat16)
-    cache_rows = jnp.concatenate([normed, key_rope], axis=-1)
-
-    page_rows = cache_rows.reshape(local_rows // block_width, block_width * cache_rows.shape[1])
-    everyone = lax.all_gather(page_rows, "req", axis=0, tiled=True)
-
-    attn_out = attention(
+    attn_out, shipped = attention(
         q_heads[0],
-        cache_rows,
-        jnp.concatenate([cosine] * 4, axis=1),
-        jnp.concatenate([-sine, sine, -sine, sine], axis=1),
+        kv_latent[0],
+        latent_gain[None],
         kv_up,
         block_order,
+        offsets,
         lengths,
+        owners,
     )
-
-    owner_here = lax.axis_index("req")
-    named_owner = owners.reshape(-1)
-    source_index = jnp.arange(named_owner.shape[0], dtype=jnp.int32)
-    matches = named_owner == owner_here
-    first_slot = jnp.min(jnp.where(matches, source_index, named_owner.shape[0]))
-    second_slot = jnp.max(jnp.where(matches, source_index, -1))
-    shipped = jnp.concatenate(
-        [
-            lax.dynamic_slice_in_dim(everyone, first_slot, 1),
-            lax.dynamic_slice_in_dim(everyone, second_slot, 1),
-        ],
-        axis=0,
-    )
-    return (attn_out[None], shipped[None])
+    return (attn_out[None], shipped.reshape(1, 2, -1))
 
 
 def solution(mesh):

time: 97.8 us -> 79.2 us (0.81)
  between operations: 19.4 us -> 1.93 us
  other arithmetic: 5.04 us -> 0 us
  Pallas kernels: 64.6 us -> 69.1 us
    pallas_call x1, Pallas kernels: 64.6 us -> 69.1 us  [attention(): pl.pallas_call(functools.partial(attention_kernel, groups, (along, across...]
    reshape x0 -> x1, local copies, waits for them, and re-layouts: none -> 1.79 us  [per_device(): return (attn_out[None], shipped.reshape(1, 2, -1))]
    unnamed x6 -> x3, local copies, waits for them, and re-layouts: 7.92 us -> 6.16 us
    reduce_min x1 -> x0, other arithmetic: 1.41 us -> none  [per_device(): first_slot = jnp.min(jnp.where(matches, source_index, named_owner.shape[0]))]
    broadcast_in_dim x1 -> x0, other arithmetic: 1 us -> none  [per_device(): return (attn_out[None], shipped[None])]
  transfers between devices with their start and end apart: 1 -> 0, of which waited for: 0 -> 0; matrix products, arithmetic and copies ran while one was open for 2% -> 0% of each run, Pallas kernels for 66% -> 0%
where the time goes in v2:
time: 79.2 us; the launch traced here: 78.9 us
  Pallas kernels  69.1 us (87%)
  local copies, waits for them, and re-layouts  7.95 us (10%)
  between operations  1.93 us (2%)
    pallas_call x1, Pallas kernels, attention(): pl.pallas_call(functools.partial(attention_kernel, groups, (along, across...  69.1 us
    unnamed x3, local copies, waits for them, and re-layouts  6.16 us
    reshape x1, local copies, waits for them, and re-layouts, per_device(): return (attn_out[None], shipped.reshape(1, 2, -1))  1.79 us

profile of v2, /device:TPU:0, one launch (start us, length us, event | category | flops | bytes accessed | tf_op | source)
XLA Modules:
  0.0 78.9 jit_solution(4524984658953460633)
XLA Ops:
  1.9 1.4 %copy.12.owners_ref = s32[16,2]{1,0:T(8,128)} copy(s32[16,2]{0,1:T(2,128)} %param.16) | data formatting | bytes 256 | tf_op args[7]
  3.3 1.7 %copy.11 = bf16[1,128,576]{2,1,0:T(8,128)(2,1)} copy(bf16[1,128,576]{1,2,0:T(8,128)(2,1)} %param.10) | data formatting | bytes 294912 | tf_op args[1]
  5.0 69.1 %shard_map.104 = (bf16[128,8192]{1,0:T(8,128)(2,1)}, bf16[2,64,576]{2,1,0:T(8,128)(2,1)}) custom-call(s32[1,4]{1,0:T(1,128)} %order_ref.1, s32[1]{0:T(128)S(6)} %copy.14.offset_ref, s32[1]{0:T(128)S(6)} %copy.15.length_ref, s32[16,2]{1,0:T(8,128)} %copy.12.owners_ref, f32[1,512]{1,0:T(1,128)} %bitcast.7, f32[1,128]{1,0:T(1,128)} %constant.2.clone.frequency_ref, ...), custom_call_target="tpu_custom_call" | custom-call | flops 4294967296 | bytes 16777216 | tf_op jit(solution)/shard_map/pallas_call | solution.py:384
  74.1 1.8 %reshape.7 = bf16[1,2,36864]{2,1,0:T(2,128)(2,1)} reshape(bf16[2,64,576]{2,1,0:T(8,128)(2,1)} %get-tuple-element.5) | data formatting | bytes 294912 | tf_op jit(solution)/shard_map/reshape | solution.py:442
  75.8 3.1 %copy.16 = bf16[1,128,8192]{2,1,0:T(8,128)(2,1)} copy(bf16[1,128,8192]{2,1,0:T(8,128)(2,1)} %bitcast.4) | data formatting | bytes 4194304
